TPU v7x, 128 devices: a whole 4x4x4 slice. The times are simulated.
128 devices in a mesh: pool: 2 (over y_lo), dp: 8 (over x, core), tp: 8 (over y_hi, z).
Axes of the slice: x: 4, y: 4 (y_hi: 2, y_lo: 2; y = y_hi * 2 + y_lo), z: 4, core: 2. Of those that a mesh axis runs over, the one named last changes fastest.
Arguments:
- hidden: bfloat16 [2, 8192, 8192], P('pool', 'dp', 'tp'), may hold values from -6 to 6
- w_kv: bfloat16 [8192, 2, 1024], P(None, None, 'tp'), may hold values from -0.0625 to 0.0625
- cache: bfloat16 [2, 32, 2048, 2, 1024], P('pool', 'dp', None, None, 'tp'), may hold values from -6 to 6
- query: bfloat16 [2, 32, 8192], P('pool', 'dp', 'tp'), may hold values from -80 to 80
- new_kv: bfloat16 [2, 32, 2, 1024], P('pool', 'dp', None, 'tp'), may hold values from -6 to 6
- lengths: int32 [2, 32], P('pool', 'dp'), may hold values from 1 to 2048
- assign: int32 [2, 8], replicated, may hold values from 0 to 31, as said below
Outputs:
- attended: bfloat16 [2, 32, 8192], P('pool', 'dp', 'tp')
Inputs may be any that keep to these rules, and one draw needn't show every extreme that they name: `assign`: the prompts of a pool name different rows; rows 0 and 31 are always named.
All inputs are finite; a program needn't handle non-finite values.
Results may differ from a plain program's by a relative error of at most 0.0045.
Values may be sent and summed in bfloat16 or wider, within the bound.
No kernel may reach another device: no remote copies, remote signals or barrier semaphores. Data moves between devices by JAX's collectives and lax.ppermute only.
A program may use at most 128 MiB of HBM per device.

v0:
```python
import jax
import jax.numpy as jnp
from jax import lax
from jax.sharding import PartitionSpec as P

HD = 128


def attend(query, keys_all, own, live, head):
    rows = query.shape[0]
    width = keys_all.shape[-1]
    kvd = width // head
    cap = keys_all.shape[1]
    groups = query.shape[1] // width
    q = query.reshape(rows, kvd, groups, head)
    k = keys_all[:, :, 0].reshape(rows, cap, kvd, head)
    v = keys_all[:, :, 1].reshape(rows, cap, kvd, head)
    own_k = own[:, 0].reshape(rows, kvd, head)
    own_v = own[:, 1].reshape(rows, kvd, head)
    scale = head ** (-0.5)
    scores = jnp.einsum("rkgd,rckd->rkgc", q, k, preferred_element_type=jnp.float32) * scale
    own_score = jnp.einsum("rkgd,rkd->rkg", q, own_k, preferred_element_type=jnp.float32) * scale
    valid = jnp.arange(cap, dtype=jnp.int32)[None, None, None, :] < live[:, None, None, None]
    masked = jnp.where(valid, scores, jnp.float32(-1e30))
    top = jnp.maximum(jnp.max(masked, axis=-1), own_score)
    weights = jnp.where(valid, jnp.exp(masked - top[..., None]), jnp.float32(0.0))
    own_weight = jnp.exp(own_score - top)
    total = jnp.sum(weights, axis=-1) + own_weight
    weights_b = weights.astype(jnp.bfloat16)
    own_b = own_weight.astype(jnp.bfloat16).astype(jnp.float32)
    mixed = jnp.einsum("rkgc,rckd->rkgd", weights_b, v, preferred_element_type=jnp.float32)
    mixed = mixed + own_b[..., None] * own_v[:, :, None, :].astype(jnp.float32)
    mixed = mixed / total[..., None]
    return mixed.reshape(rows, kvd * groups * head).astype(jnp.bfloat16)


def per_device(hidden, w_kv, cache, query, new_kv, lengths, assign):
    local = hidden[0]
    plen = local.shape[0]
    width = w_kv.shape[2]
    piece = lax.all_gather(local, "tp", axis=1, tiled=True)
    rows_w = w_kv.reshape(piece.shape[1], 2 * width)
    projected = jnp.dot(piece, rows_w, preferred_element_type=jnp.float32)
    block = projected.astype(jnp.bfloat16).reshape(plen, 2, width)
    other = 1 - lax.axis_index("pool")
    groups_dp = lax.axis_size("dp")
    rows_dev = cache.shape[1]
    row_list = lax.dynamic_index_in_dim(assign, other, 0, keepdims=False)
    row_ids = lax.axis_index("dp") * rows_dev + jnp.arange(rows_dev, dtype=jnp.int32)
    match = row_list[None, :] == row_ids[:, None]
    taken = jnp.any(match, axis=1)
    everything = lax.all_gather(block[None], ("pool", "dp"), axis=0, tiled=True)
    prompts = lax.dynamic_slice_in_dim(everything, other * groups_dp, groups_dp, 0)
    picked = jnp.dot(
        match.astype(jnp.bfloat16),
        prompts.reshape(groups_dp, plen * 2 * width),
        preferred_element_type=jnp.float32,
    )
    picked = picked.astype(jnp.bfloat16).reshape(rows_dev, plen, 2, width)
    resident = cache[0]
    front = jnp.where(taken[:, None, None, None], picked, resident[:, :plen])
    keys_all = jnp.concatenate([front, resident[:, plen:]], axis=1)
    live = jnp.where(taken, jnp.int32(plen), lengths[0])
    head = HD
    return attend(query[0], keys_all, new_kv[0], live, head)[None]


def solution(mesh):
    placed = (
        P("pool", "dp", "tp"),
        P(None, None, "tp"),
        P("pool", "dp", None, None, "tp"),
        P("pool", "dp", "tp"),
        P("pool", "dp", None, "tp"),
        P("pool", "dp"),
        P(),
    )
    return jax.shard_map(
        per_device, mesh=mesh, in_specs=placed, out_specs=P("pool", "dp", "tp"), check_vma=False
    )
```

profile of v0, /device:TPU:1, one launch (start us, length us, event | category | flops | bytes accessed | tf_op | source)
XLA Modules:
  0.0 292.0 jit_solution(12973785671193936706)
XLA Ops:
  6.5 0.0 copy-start
  6.5 0.0 all-gather.6.cloned.1.call-start
  6.5 0.7 all-gather.6.cloned.1.call-update
  7.3 0.0 all-gather.4.cloned.1.call-start
  7.3 188.1 %all-gather.6.cloned.1.call-done = bf16[1,1024,8192]{2,1,0:T(8,128)(2,1)} async-done(((bf16[1,1024,1024]{2,1,0:T(8,128)(2,1)}), bf16[1,1024,8192]{2,1,0:T(8,128)(2,1)}) %all-gather.6.cloned.1.call-update) | async-done | bytes 16777232 | tf_op jit(solution)/shard_map/all_gather | solution.py:41
  195.5 9.5 %fusion.13 = bf16[1024,256]{0,1:T(8,128)(2,1)S(1)} fusion(bf16[1024,8,2,128]{3,2,1,0:T(2,128)(2,1)} %bitcast.59, bf16[1,1024,8192]{2,1,0:T(8,128)(2,1)} %all-gather.6.cloned.1.call-done), kind=kOutput, calls=%fused_computation.18 | convolution fusion | flops 4295229440 | bytes 21495808 | tf_op jit(solution)/shard_map/dot_general | solution.py:43
  205.0 1.0 copy.17
  206.0 0.0 all-gather.4.cloned.1.call-update
  206.0 0.0 copy-start.3
  206.1 0.0 copy-start.1
  206.1 0.0 copy-start.2
  206.1 4.7 %copy.43 = bf16[1,4,2048,2,128]{4,2,1,3,0:T(8,128)(2,1)} copy(bf16[1,4,2048,2,128]{4,3,2,1,0:T(2,128)(2,1)} %param.9) | data formatting | bytes 8388608 | tf_op args[2]
  210.8 0.0 copy-done
  210.8 0.2 compare_reduce_fusion
  211.0 0.0 copy-done.3
  211.0 0.0 copy-done.1
  211.0 0.0 copy-done.2
  211.0 0.1 fusion.33
  211.1 0.1 iota_compare_fusion
  211.2 45.6 %all-gather.4.cloned.1.call-done = bf16[16,1024,2,128]{3,1,2,0:T(8,128)(2,1)} async-done(((bf16[1,1024,2,128]{3,1,2,0:T(8,128)(2,1)}), bf16[16,1024,2,128]{3,1,2,0:T(8,128)(2,1)}) %all-gather.4.cloned.1.call-update) | async-done | bytes 8388624 | tf_op jit(solution)/shard_map/all_gather | solution.py:52
  256.8 2.5 constant_dynamic-slice_fusion
  259.3 6.3 %copy.18 = bf16[8,1024,2,128]{3,2,1,0:T(2,128)(2,1)} copy(bf16[8,1024,2,128]{3,1,2,0:T(8,128)(2,1)S(1)} %constant_dynamic-slice_fusion) | data formatting | bytes 8388608 | tf_op jit(solution)/shard_map/dynamic_slice | solution.py:53
  265.6 7.3 %reshape.124 = bf16[8,262144]{1,0:T(8,128)(2,1)} reshape(bf16[8,1024,2,128]{3,2,1,0:T(2,128)(2,1)} %copy.18) | data formatting | bytes 8388608 | tf_op jit(solution)/shard_map/reshape | solution.py:56
  272.9 3.5 %convolution_convert_fusion = bf16[4,262144]{1,0:T(4,128)(2,1)S(1)} fusion(bf16[8,262144]{1,0:T(8,128)(2,1)} %reshape.124, s32[8]{0:T(128)S(1)} %dynamic-slice_bitcast_fusion, s32[4]{0:T(128)S(1)} %iota_add_fusion), kind=kOutput, calls=%fused_computation | convolution fusion | flops 17825824 | bytes 6291504 | tf_op jit(solution)/shard_map/dot_general | solution.py:54
  276.4 3.4 %reshape.125 = bf16[4,1024,2,128]{3,2,1,0:T(2,128)(2,1)} reshape(bf16[4,262144]{1,0:T(4,128)(2,1)S(1)} %convolution_convert_fusion) | data formatting | bytes 4194304 | tf_op jit(solution)/shard_map/reshape | solution.py:59
  279.8 3.3 %slice_select_fusion = (bf16[4,1024,2,128]{3,1,0,2:T(8,128)(2,1)S(1)}, bf16[4,1024,2,128]{3,1,0,2:T(8,128)(2,1)S(1)}) fusion(bf16[4,2048,2,128]{3,1,0,2:T(8,128)(2,1)} %bitcast.52, bf16[4,1024,2,128]{3,2,1,0:T(2,128)(2,1)} %reshape.125, pred[4]{0:T(512)(128)(4,1)S(1)} %compare_reduce_fusion), kind=kLoop, calls=%fused_computation.17 | loop fusion | flops 1048576 | bytes 10485764 | tf_op jit(solution)/shard_map/jit(_where)/select_n | solution.py:61
  283.1 0.7 fusion.45
  283.9 0.2 fusion.27
  284.1 0.5 fusion.24
  284.6 0.6 convert_element_type.51
  (6 shorter events, 0.0 us)
Async XLA Ops:
  6.5 204.2 %copy-start = (s32[2,8]{1,0:T(2,128)S(1)}, s32[2,8]{1,0:T(2,128)}, u32[]{:S(2)}) copy-start(s32[2,8]{1,0:T(2,128)} %param.13) | copy-start | bytes 196
  6.5 188.9 %all-gather.6.cloned.1.call-start = ((), (), s32[]{:S(2)}) async-start(), calls=%async_computation.1 | async-start | bytes 18874368 | tf_op jit(solution)/shard_map/all_gather | solution.py:41
  7.3 249.6 %all-gather.4.cloned.1.call-start = ((), (), s32[]{:S(2)}) async-start(), calls=%async_computation | async-start | bytes 8912896 | tf_op jit(solution)/shard_map/all_gather | solution.py:52
  206.0 4.9 %copy-start.3 = (s32[1,4]{1,0:T(1,128)S(1)}, s32[1,4]{1,0:T(1,128)}, u32[]{:S(2)}) copy-start(s32[1,4]{1,0:T(1,128)} %param.12) | copy-start | bytes 52
  206.1 4.9 %copy-start.1 = (bf16[1,4,2,128]{3,2,1,0:T(2,128)(2,1)S(1)}, bf16[1,4,2,128]{3,2,1,0:T(2,128)(2,1)}, u32[]{:S(2)}) copy-start(bf16[1,4,2,128]{3,2,1,0:T(2,128)(2,1)} %param.11) | copy-start | bytes 6148
  206.1 4.9 %copy-start.2 = (bf16[1,4,1024]{2,1,0:T(4,128)(2,1)S(1)}, bf16[1,4,1024]{2,1,0:T(4,128)(2,1)}, u32[]{:S(2)}) copy-start(bf16[1,4,1024]{2,1,0:T(4,128)(2,1)} %param.10) | copy-start | bytes 24580
Sparse Core Ops, SparseCore 0:
  9.7 185.7 all-gather.5
  206.2 50.6 all-gather.3
where the time goes:
time: 292 us
  waiting for transfers between devices  234 us (80%)
  local copies, waits for them, and re-layouts  25.8 us (9%)
  matrix products  14.3 us (5%)
  between operations  13.5 us (5%)
  other arithmetic  3.84 us (1%)
    all_gather x1, waiting for transfers between devices, per_device(): piece = lax.all_gather(local, 'tp', axis=1, tiled=True)  188 us
    all_gather x1, waiting for transfers between devices, per_device(): everything = lax.all_gather(block[None], ('pool', 'dp'), axis=0, tiled=True)  45.6 us
    dot_general x1, matrix products, per_device(): projected = jnp.dot(piece, rows_w, preferred_element_type=jnp.float32)  9.53 us
    dynamic_slice x2, local copies, waits for them, and re-layouts, per_device(): lax.dynamic_slice_in_dim(everything, other * groups_dp, groups_dp, 0)  8.74 us
    reshape x1, local copies, waits for them, and re-layouts, per_device(): prompts.reshape(groups_dp, plen * 2 * width)  7.33 us
  transfers between devices with their start and end apart: 2, of which 2 were waited for; matrix products, arithmetic and copies ran while one was open for 2% of the time, Pallas kernels for 0%

commit v1 on v0

v1 whole, which is shorter than its diff:
```python
import functools

import jax
import jax.numpy as jnp
from jax import lax
from jax.experimental import pallas as pl
from jax.experimental.pallas import tpu as pltpu
from jax.sharding import PartitionSpec as P

HD = 128
F32 = jnp.float32
BF16 = jnp.bfloat16
NEG = -1e30


def nt(a, b):
    return lax.dot_general(a, b, (((1,), (1,)), ((), ())), preferred_element_type=F32)


def nn(a, b):
    return jnp.dot(a, b, preferred_element_type=F32)


def split(x):
    hi = x.astype(BF16)
    lo = (x - hi.astype(F32)).astype(BF16)
    return hi, lo


def heads_of(row, groups):
    return jnp.concatenate([row[:, h * HD:(h + 1) * HD] for h in range(groups)], axis=0)


def spread(rows, cols, odd):
    r = lax.broadcasted_iota(jnp.int32, (rows, cols), 0)
    c = lax.broadcasted_iota(jnp.int32, (rows, cols), 1)
    return jnp.where(r == 2 * c + odd, 1.0, 0.0).astype(F32).astype(BF16)


def gather_t(rows, cols, odd):
    r = lax.broadcasted_iota(jnp.int32, (rows, cols), 0)
    c = lax.broadcasted_iota(jnp.int32, (rows, cols), 1)
    return jnp.where(c == 2 * r + odd, 1.0, 0.0).astype(F32).astype(BF16)


def own_of(packed):
    q = packed[0:8]
    k = packed[8:9]
    v = packed[9:10]
    return jnp.sum(q * k, axis=1, keepdims=True) * (HD ** -0.5), v


def send_kernel(meta, assign, query, own, out):
    other, g = 1 - meta[0], meta[1]
    rows = query.shape[0]
    n = assign.shape[1]
    q = query[...].astype(F32)
    kv = own[...].astype(F32)
    packed = []
    for j in range(rows):
        mine = heads_of(q[j:j + 1], q.shape[1] // HD)
        pad = jnp.zeros((16 - mine.shape[0] - 2, HD), F32)
        packed.append(jnp.concatenate([mine, kv[2 * j:2 * j + 2], pad], axis=0))
    for i in range(n):
        at = assign[other, i] - g * rows
        value = packed[0]
        for j in range(1, rows):
            value = jnp.where(at == j, packed[j], value)
        value = value.astype(BF16)
        out[i] = value
        out[n + i] = value


def source(meta, assign):
    me, g = meta[0], meta[1]
    return (1 - me) * assign.shape[1] + assign[me, g] // meta[2]


def fold_kernel(meta, assign, got, w_low, w_high, out):
    q = got[source(meta, assign)][0:8]
    dloc = w_low.shape[0] // 2
    even = spread(256, 128, 0)
    for part, w in enumerate((w_low, w_high)):
        wide = nt(q, w[...])
        hi, lo = split(wide)
        both = jnp.concatenate([hi, lo], axis=0)
        blocks = both.shape[1] // 256
        tall = jnp.concatenate([both[:, b * 256:(b + 1) * 256] for b in range(blocks)], axis=0)
        kept = nn(tall, even)
        value = jnp.concatenate(
            [kept[b * 16:b * 16 + 8] + kept[b * 16 + 8:b * 16 + 16] for b in range(blocks)], axis=1
        )
        for copy in range(out.shape[0]):
            out[copy, 0, :, part * dloc:(part + 1) * dloc] = value


def score_kernel(meta, qs, h, hx, out):
    n, heads, wide = qs.shape
    d = wide // 2
    y = meta[3]
    toks = out.shape[1]

    def term(at, rows):
        q = qs[:, :, pl.ds(pl.multiple_of(at * d, d), d)].reshape(n * heads, d)
        hi, lo = split(q)
        both = nt(jnp.concatenate([hi, lo], axis=0), rows)
        return both[:n * heads] + both[n * heads:]

    mine = h[pl.ds(pl.multiple_of(y * toks, toks), toks), :]
    out[...] = term(y, mine) + term(1 - y, hx[...])


def mix_kernel(meta, left, right, h, hx, out):
    n, heads, wide = out.shape
    d = (wide - HD) // 2
    y = meta[3]
    rows, toks = left.shape
    s = (left[...] + right[...]) * (HD ** -0.5)
    top = jnp.max(s, axis=1, keepdims=True)
    weights = jnp.exp(s - top)
    total = jnp.sum(weights, axis=1, keepdims=True)
    hi, lo = split(weights)
    both = jnp.concatenate([hi, lo], axis=0)

    def term(at, values):
        mixed = nn(both, values)
        mixed = (mixed[:rows] + mixed[rows:]).reshape(n, heads, d)
        out[:, :, pl.ds(pl.multiple_of(at * d, d), d)] = mixed

    term(y, h[pl.ds(pl.multiple_of(y * toks, toks), toks), :])
    term(1 - y, hx[...])
    lane = lax.broadcasted_iota(jnp.int32, (rows, HD), 1)
    tail = jnp.where(lane == 0, top, total)
    out[:, :, 2 * d:] = tail.reshape(n, heads, HD)


def value_kernel(meta, assign, got, mixed, w_low, w_high, out, acc, top_ref, total_ref):
    step = pl.program_id(0)
    heads, wide = mixed.shape[2], mixed.shape[3]
    d = (wide - HD) // 2
    tops = [mixed[y, 0, :, 2 * d:2 * d + 1] for y in range(2)]

    @pl.when(step == 0)
    def _():
        own_score, own_v = own_of(got[source(meta, assign)].astype(F32))
        top = jnp.maximum(jnp.maximum(tops[0], tops[1]), own_score)
        own_weight = jnp.exp(own_score - top)
        total = own_weight
        for y in range(2):
            total = total + jnp.exp(tops[y] - top) * mixed[y, 0, :, 2 * d + 1:2 * d + 2]
        acc[0:heads] = own_weight.astype(BF16).astype(F32) * own_v
        acc[heads:] = jnp.zeros((heads, HD), F32)
        top_ref[...] = jnp.broadcast_to(top, top_ref.shape)
        total_ref[...] = jnp.broadcast_to(total, total_ref.shape)

    top = top_ref[:, 0:1]
    both = jnp.exp(tops[0] - top) * mixed[0, 0, :, :2 * d] + jnp.exp(tops[1] - top) * mixed[1, 0, :, :2 * d]
    hi, lo = split(both)
    both = jnp.concatenate([hi, lo], axis=0)
    odd = gather_t(128, 256, 1)
    for part, w in enumerate((w_low, w_high)):
        half = both[:, part * d:(part + 1) * d]
        blocks = d // 128
        tall = jnp.concatenate([half[:, b * 128:(b + 1) * 128] for b in range(blocks)], axis=0)
        spaced = nn(tall, odd).astype(BF16)
        flat = jnp.concatenate([spaced[b * 16:(b + 1) * 16] for b in range(blocks)], axis=1)
        acc[...] += nn(flat, w[...])

    @pl.when(step == pl.num_programs(0) - 1)
    def _():
        done = (acc[0:heads] + acc[heads:]) / total_ref[...]
        for j in range(out.shape[0]):
            out[j] = done


def resident_kernel(first, lengths, query, own, kv, out):
    j = pl.program_id(0) + first
    live = lengths[j]
    rows = query.shape[0]
    wide = query[...].astype(F32)
    pairs = own[...].astype(F32)
    row = wide[0:1]
    ok = pairs[0:1]
    ov = pairs[1:2]
    for r in range(1, rows):
        row = jnp.where(j == r, wide[r:r + 1], row)
        ok = jnp.where(j == r, pairs[2 * r:2 * r + 1], ok)
        ov = jnp.where(j == r, pairs[2 * r + 1:2 * r + 2], ov)
    q = heads_of(row, query.shape[1] // HD)
    own_score = jnp.sum(q * ok, axis=1, keepdims=True) * (HD ** -0.5)
    s = nt(q.astype(BF16), kv[0]) * (HD ** -0.5)
    at = lax.broadcasted_iota(jnp.int32, s.shape, 1)
    valid = (at < 2 * live) & (at % 2 == 0)
    s = jnp.where(valid, s, NEG)
    top = jnp.maximum(jnp.max(s, axis=1, keepdims=True), own_score)
    weights = jnp.where(valid, jnp.exp(s - top), 0.0)
    own_weight = jnp.exp(own_score - top)
    total = jnp.sum(weights, axis=1, keepdims=True) + own_weight
    shifted = pltpu.roll(weights, 1, 1).astype(BF16)
    mixed = nn(shifted, kv[0]) + own_weight.astype(BF16).astype(F32) * ov
    out[0] = mixed / total


def merge_kernel(meta, assign, got, *refs):
    out = refs[-1]
    other, g = 1 - meta[0], meta[1]
    n = assign.shape[1]
    here = [part[k] for part in refs[:-1] for k in range(part.shape[0])]
    rows = []
    for j, value in enumerate(here):
        for i in range(n):
            value = jnp.where(assign[other, i] == g * len(here) + j, got[other * n + i], value)
        rows.append(jnp.concatenate([value[h:h + 1] for h in range(value.shape[0])], axis=1))
    out[...] = jnp.concatenate(rows, axis=0).astype(BF16)


SMEM = pl.BlockSpec(memory_space=pltpu.SMEM)
VMEM = pl.BlockSpec(memory_space=pltpu.VMEM)
MIB = 1024 * 1024


def shaped(shape, dtype):
    return jax.ShapeDtypeStruct(shape, dtype)


def call(kernel, limit, **kw):
    return pl.pallas_call(
        kernel, compiler_params=pltpu.CompilerParams(vmem_limit_bytes=limit * MIB), **kw
    )


def per_device(hidden, w_kv, cache, query, new_kv, lengths, assign):
    h = hidden[0]
    plen, dloc = h.shape
    rows, cap = cache.shape[1], cache.shape[2]
    heads = query.shape[2] // HD
    n_tp = lax.axis_size("tp")
    n_z = n_tp // 2
    n_all = 2 * lax.axis_size("dp")
    toks = plen // 2
    y = lax.axis_index("tp") // n_z
    meta = jnp.stack([lax.axis_index("pool"), lax.axis_index("dp"), rows, y]).astype(jnp.int32)
    w = w_kv.reshape(w_kv.shape[0] * 2, HD)
    kv = cache.reshape(rows, cap * 2, HD)
    q_rows = query[0]
    own = new_kv[0].reshape(rows * 2, HD)

    across = [(i, (i + n_z) % n_tp) for i in range(n_tp)]
    theirs = lax.dynamic_slice_in_dim(h, (1 - y) * toks, toks, 0)
    hx = lax.ppermute(theirs, "tp", across)

    sent = call(
        send_kernel,
        56,
        out_shape=shaped((n_all, 16, HD), BF16),
        in_specs=[SMEM, SMEM, VMEM, VMEM],
        out_specs=VMEM,
        name="send",
    )(meta, assign, q_rows, own)
    got = lax.all_to_all(sent, ("pool", "dp"), 0, 0, tiled=True)

    w_low = pl.BlockSpec((2 * dloc, HD), lambda i: (i, 0))
    w_high = pl.BlockSpec((2 * dloc, HD), lambda i: (i + n_z, 0))
    folded = call(
        fold_kernel,
        56,
        grid=(n_z,),
        out_shape=shaped((2, n_z, heads, 2 * dloc), F32),
        in_specs=[SMEM, SMEM, VMEM, w_low, w_high],
        out_specs=pl.BlockSpec((2, 1, heads, 2 * dloc), lambda i: (0, i, 0, 0)),
        name="fold",
    )(meta, assign, got, w, w)
    folded = folded.reshape(n_tp, heads, 2 * dloc)
    folded = lax.all_to_all(folded, "tp", 0, 0, tiled=True)

    score = call(
        score_kernel,
        24,
        out_shape=shaped((n_tp * heads, toks), F32),
        in_specs=[SMEM, VMEM, VMEM, VMEM],
        out_specs=VMEM,
        name="score",
    )(meta, folded, h, hx)
    near = [(i, i ^ 1) for i in range(n_tp)]
    far = [(i, i ^ 2) for i in range(n_tp)]
    score = score + lax.ppermute(score, "tp", near)
    twin = lax.ppermute(score, "tp", far)

    halves = []
    for first in range(0, rows, 2):
        halves.append(
            call(
                functools.partial(resident_kernel, first),
                24,
                grid=(2,),
                out_shape=shaped((2, heads, HD), F32),
                in_specs=[
                    SMEM,
                    VMEM,
                    VMEM,
                    pl.BlockSpec((1, cap * 2, HD), lambda i, first=first: (i + first, 0, 0)),
                ],
                out_specs=pl.BlockSpec((1, heads, HD), lambda i: (i, 0, 0)),
                name="resident",
                cost_estimate=pl.CostEstimate(
                    flops=2 * 2 * 16 * cap * 2 * HD * 2, bytes_accessed=2 * cap * 2 * HD * 2, transcendentals=0
                ),
            )(lengths[0], q_rows, own, kv)
        )

    mixed = call(
        mix_kernel,
        24,
        out_shape=shaped((n_tp, heads, 2 * dloc + HD), F32),
        in_specs=[SMEM, VMEM, VMEM, VMEM, VMEM],
        out_specs=VMEM,
        name="mix",
    )(meta, score, twin, h, hx)
    mixed = lax.all_to_all(mixed, "tp", 0, 0, tiled=True)

    done = call(
        value_kernel,
        24,
        grid=(n_z,),
        out_shape=shaped((n_all, heads, HD), F32),
        in_specs=[
            SMEM,
            SMEM,
            VMEM,
            pl.BlockSpec((2, 1, heads, 2 * dloc + HD), lambda i: (0, i, 0, 0)),
            w_low,
            w_high,
        ],
        out_specs=VMEM,
        scratch_shapes=[
            pltpu.VMEM((2 * heads, HD), F32),
            pltpu.VMEM((heads, HD), F32),
            pltpu.VMEM((heads, HD), F32),
        ],
        name="value",
    )(meta, assign, got, mixed.reshape(2, n_z, heads, 2 * dloc + HD), w, w)
    done = lax.all_to_all(done, ("pool", "dp"), 0, 0, tiled=True)

    merged = call(
        merge_kernel,
        56,
        out_shape=shaped((rows, heads * HD), BF16),
        in_specs=[SMEM, SMEM] + [VMEM] * (1 + len(halves)),
        out_specs=VMEM,
        name="merge",
    )(meta, assign, done, *halves)
    return merged[None]


def solution(mesh):
    placed = (
        P("pool", "dp", "tp"),
        P(None, None, "tp"),
        P("pool", "dp", None, None, "tp"),
        P("pool", "dp", "tp"),
        P("pool", "dp", None, "tp"),
        P("pool", "dp"),
        P(),
    )
    return jax.shard_map(
        per_device, mesh=mesh, in_specs=placed, out_specs=P("pool", "dp", "tp"), check_vma=False
    )
```

time: 292 us -> 99.7 us (0.34)
  waiting for transfers between devices: 234 us -> 7.56 us
  blocking collectives: 0 us -> 52.4 us
  local copies, waits for them, and re-layouts: 25.8 us -> 5.34 us
  Pallas kernels: 0 us -> 18.5 us
  starting transfers between devices: 0.04 us -> 14.6 us
  matrix products: 14.3 us -> 0 us
  between operations: 13.5 us -> 0.15 us
  other arithmetic: 3.84 us -> 0.66 us
    all_gather x2 -> x0, waiting for transfers between devices: 234 us -> none  [the longest x1 188 us: per_device(): piece = lax.all_gather(local, 'tp', axis=1, tiled=True)]
    all_to_all x0 -> x3, blocking collectives: none -> 52.4 us  [the longest x1 22.9 us: per_device(): got = lax.all_to_all(sent, ('pool', 'dp'), 0, 0, tiled=True)]
    pallas_call x0 -> x8, Pallas kernels: none -> 18.5 us  [the longest x1 5.2 us: per_device(): call(fold_kernel, 56, grid=(n_z,), out_shape=shaped((2, n_z, heads, 2 * d...]
    dot_general x5 -> x0, matrix products: 14.3 us -> none  [the longest x1 9.53 us: per_device(): projected = jnp.dot(piece, rows_w, preferred_element_type=jnp.float32)]
    reshape x2 -> x0, local copies, waits for them, and re-layouts: 10.8 us -> none  [the longest x1 7.33 us: per_device(): prompts.reshape(groups_dp, plen * 2 * width)]
    all_to_all x0 -> x1, starting transfers between devices: none -> 9.06 us  [per_device(): done = lax.all_to_all(done, ('pool', 'dp'), 0, 0, tiled=True)]
    ppermute x0 -> x3, waiting for transfers between devices: none -> 7.56 us  [the longest x1 3.8 us: per_device(): score = score + lax.ppermute(score, 'tp', near)]
    dynamic_slice x2 -> x1, local copies, waits for them, and re-layouts: 8.74 us -> 1.29 us  [per_device(): theirs = lax.dynamic_slice_in_dim(h, (1 - y) * toks, toks, 0)]
  transfers between devices with their start and end apart: 2 -> 4, of which waited for: 2 -> 2; matrix products, arithmetic and copies ran while one was open for 2% -> 1% of each run, Pallas kernels for 0% -> 10%
where the time goes in v1:
time: 99.7 us; the launch traced here: 99.2 us
  blocking collectives  52.4 us (53%)
  Pallas kernels  18.5 us (19%)
  starting transfers between devices  14.6 us (15%)
  waiting for transfers between devices  7.56 us (8%)
  local copies, waits for them, and re-layouts  5.34 us (5%)
    all_to_all x1, blocking collectives, per_device(): got = lax.all_to_all(sent, ('pool', 'dp'), 0, 0, tiled=True)  22.9 us
    all_to_all x1, blocking collectives, per_device(): folded = lax.all_to_all(folded, 'tp', 0, 0, tiled=True)  16.3 us
    all_to_all x1, blocking collectives, per_device(): mixed = lax.all_to_all(mixed, 'tp', 0, 0, tiled=True)  13.2 us
    all_to_all x1, starting transfers between devices, per_device(): done = lax.all_to_all(done, ('pool', 'dp'), 0, 0, tiled=True)  9.06 us
    pallas_call x1, Pallas kernels, per_device(): call(fold_kernel, 56, grid=(n_z,), out_shape=shaped((2, n_z, heads, 2 * d...  5.2 us
    pallas_call x2, Pallas kernels, per_device(): call(functools.partial(resident_kernel, first), 24, grid=(2,), out_shape=...  4.26 us
    unnamed x24, local copies, waits for them, and re-layouts  4.04 us
    ppermute x1, starting transfers between devices, per_device(): hx = lax.ppermute(theirs, 'tp', across)  3.82 us
  transfers between devices with their start and end apart: 4, of which 2 were waited for; matrix products, arithmetic and copies ran while one was open for 1% of the time, Pallas kernels for 10%

profile of v1, /device:TPU:1, one launch (start us, length us, event | category | flops | bytes accessed | tf_op | source)
XLA Modules:
  0.0 99.2 jit_solution(8100888416337672228)
XLA Ops:
  0.0 1.3 %dynamic-slice_bitcast_fusion = bf16[512,1024]{1,0:T(8,128)(2,1)S(1)} fusion(bf16[1,1024,1024]{2,1,0:T(8,128)(2,1)} %param.7, s32[]{:T(128)S(6)} %select_n.9), kind=kLoop, calls=%fused_computation | loop fusion | bytes 2097156 | tf_op jit(solution)/shard_map/dynamic_slice | solution.py:249
  1.3 3.8 %collective-permute-start = (bf16[512,1024]{1,0:T(8,128)(2,1)S(1)}, bf16[512,1024]{1,0:T(8,128)(2,1)S(1)}, u32[]{:S(2)}, u32[]{:S(2)}) collective-permute-start(bf16[512,1024]{1,0:T(8,128)(2,1)S(1)} %dynamic-slice_bitcast_fusion), channel_id=1, source_target_pairs={{0,4},{1,5},{2,6},{3,7},{4,0},{5,1},{6,2},{7,3},{8,12},{9,13},{10,... | collective-permute-start | bytes 3145736 | tf_op jit(solution)/shard_map/ppermute | solution.py:250
  5.1 0.6 pad_add_fusion.meta
  5.8 1.4 %send.1 = bf16[16,16,128]{2,1,0:T(8,128)(2,1)} custom-call(s32[4]{0:T(128)} %pad_add_fusion.meta, s32[2,8]{1,0:T(2,128)} %assign.7, bf16[4,1024]{1,0:T(4,128)(2,1)} %bitcast.23, bf16[8,128]{1,0:T(8,128)(2,1)} %bitcast.26), custom_call_target="tpu_custom_call" | custom-call | tf_op jit(solution)/shard_map/send/pallas_call | solution.py:252
  7.1 22.9 %all_to_all.20.got = bf16[16,16,128]{2,1,0:T(8,128)(2,1)} all-to-all(bf16[16,16,128]{2,1,0:T(8,128)(2,1)} %send.1), channel_id=1, replica_groups=mesh['pool'=2,'dp'=8,'tp'=8] {'pool','dp'}, dimensions={0} | all-to-all | bytes 131072 | tf_op jit(solution)/shard_map/all_to_all | solution.py:260
  30.0 0.0 copy-start.2
  30.0 0.0 copy-start.7
  30.0 5.2 %fold.1 = f32[2,4,8,2048]{3,2,1,0:T(8,128)} custom-call(s32[4]{0:T(128)} %pad_add_fusion.meta, s32[2,8]{1,0:T(2,128)} %assign.7, bf16[16,16,128]{2,1,0:T(8,128)(2,1)} %all_to_all.20.got, bf16[16384,128]{1,0:T(8,128)(2,1)} %bitcast.14, bf16[16384,128]{1,0:T(8,128)(2,1)} %bitcast.15), custom_call_target="tpu_custom_call" | custom-call | tf_op jit(solution)/shard_map/fold/pallas_call | solution.py:264
  35.2 16.3 %all_to_all.21.qs = f32[8,8,2048]{2,1,0:T(8,128)S(1)} all-to-all(f32[8,8,2048]{2,1,0:T(8,128)} %bitcast.31), channel_id=1, replica_groups=mesh['pool'=2,'dp'=8,'tp'=8] {'tp'}, dimensions={0} | all-to-all | bytes 1048576 | tf_op jit(solution)/shard_map/all_to_all | solution.py:274
  51.5 0.0 collective-permute-done.hx
  51.5 0.0 copy-done.2
  51.5 0.0 copy-done.7
  51.5 0.0 copy-start
  51.5 0.0 copy-start.3
  51.5 0.0 copy-start.9
  51.5 1.4 %score.1 = f32[64,512]{1,0:T(8,128)S(1)} custom-call(s32[4]{0:T(128)S(1)} %copy-done.7, f32[8,8,2048]{2,1,0:T(8,128)S(1)} %all_to_all.21.qs, bf16[1024,1024]{1,0:T(8,128)(2,1)S(1)} %bitcast.20, bf16[512,1024]{1,0:T(8,128)(2,1)S(1)} %collective-permute-done.hx), custom_call_target="tpu_custom_call" | custom-call | tf_op jit(solution)/shard_map/score/pallas_call | solution.py:276
  52.9 0.1 collective-permute-start.1
  53.0 3.8 %collective-permute-done.1 = f32[64,512]{1,0:T(8,128)S(1)} collective-permute-done((f32[64,512]{1,0:T(8,128)S(1)}, f32[64,512]{1,0:T(8,128)S(1)}, u32[]{:S(2)}, u32[]{:S(2)}) %collective-permute-start.1) | collective-permute-done | bytes 131104 | tf_op jit(solution)/shard_map/ppermute | solution.py:286
  56.9 1.7 %collective-permute-start.2 = (f32[64,512]{1,0:T(8,128)S(1)}, f32[64,512]{1,0:T(8,128)S(1)}, u32[]{:S(2)}, u32[]{:S(2)}) collective-permute-start(f32[64,512]{1,0:T(8,128)S(1)} %add.8.left), channel_id=1, source_target_pairs={{0,2},{1,3},{2,0},{3,1},{4,6},{5,7},{6,4},{7,5},{8,10},{9,11},{10,... | collective-permute-start | bytes 393224 | tf_op jit(solution)/shard_map/ppermute | solution.py:287
  58.5 3.8 %collective-permute-done.2.right = f32[64,512]{1,0:T(8,128)S(1)} collective-permute-done((f32[64,512]{1,0:T(8,128)S(1)}, f32[64,512]{1,0:T(8,128)S(1)}, u32[]{:S(2)}, u32[]{:S(2)}) %collective-permute-start.2) | collective-permute-done | bytes 131104 | tf_op jit(solution)/shard_map/ppermute | solution.py:287
  62.3 1.0 %mix.1 = f32[8,8,2176]{2,1,0:T(8,128)S(1)} custom-call(s32[4]{0:T(128)S(1)} %copy-done.7, f32[64,512]{1,0:T(8,128)S(1)} %add.8.left, f32[64,512]{1,0:T(8,128)S(1)} %collective-permute-done.2.right, bf16[1024,1024]{1,0:T(8,128)(2,1)S(1)} %bitcast.21, bf16[512,1024]{1,0:T(8,128)(2,1)S(1)} %collective-permute-done.hx), custom_call_target="tpu_custom_call" | custom-call | tf_op jit(solution)/shard_map/mix/pallas_call | solution.py:311
  63.3 13.2 %all_to_all.22 = f32[8,8,2176]{2,1,0:T(8,128)S(1)} all-to-all(f32[8,8,2176]{2,1,0:T(8,128)S(1)} %mix.1), channel_id=1, replica_groups=mesh['pool'=2,'dp'=8,'tp'=8] {'tp'}, dimensions={0} | all-to-all | bytes 1114112 | tf_op jit(solution)/shard_map/all_to_all | solution.py:319
  76.5 0.0 copy-done
  76.5 0.0 copy-done.3
  76.5 0.0 copy-done.9
  76.5 0.0 copy-start.4
  76.5 0.0 copy-start.8
  76.5 0.0 copy-start.10
  76.6 3.7 %value.1 = f32[16,8,128]{2,1,0:T(8,128)} custom-call(s32[4]{0:T(128)S(1)} %copy-done.7, s32[2,8]{1,0:T(2,128)S(1)} %copy-done.9, bf16[16,16,128]{2,1,0:T(8,128)(2,1)S(1)} %copy-done.3, f32[2,4,8,2176]{3,2,1,0:T(8,128)S(1)} %bitcast.22, bf16[16384,128]{1,0:T(8,128)(2,1)S(1)} %bitcast.16, bf16[16384,128]{1,0:T(8,128)(2,1)S(1)} %bitcast.17), custom_call_target="tpu_custom_call" | custom-call | tf_op jit(solution)/shard_map/value/pallas_call | solution.py:321
  80.3 9.1 %all-to-all-start.3 = ((f32[16,8,128]{2,1,0:T(8,128)}), f32[16,8,128]{2,1,0:T(8,128)S(1)}, u32[]{:S(2)}, u32[]{:S(2)}) async-start(f32[16,8,128]{2,1,0:T(8,128)} %value.1), calls=%async_computation.3 | async-start | bytes 131072 | tf_op jit(solution)/shard_map/all_to_all | solution.py:342
  89.3 0.0 copy-done.4
  89.3 0.0 copy-done.8
  89.3 0.0 copy-done.10
  89.4 0.0 copy-start.1
  89.4 2.2 %copy-done.1 = bf16[1,4,2048,2,128]{4,3,2,1,0:T(2,128)(2,1)S(1)} copy-done((bf16[1,4,2048,2,128]{4,3,2,1,0:T(2,128)(2,1)S(1)}, bf16[1,4,2048,2,128]{4,3,2,1,0:T(2,128)(2,1)}, u32[]{:S(2)}) %copy-start.1) | copy-done | bytes 4194328
  91.5 2.1 %resident.2.refs_0_ = f32[2,8,128]{2,1,0:T(8,128)S(1)} custom-call(s32[4]{0:T(128)S(1)} %bitcast.29, bf16[4,1024]{1,0:T(4,128)(2,1)S(1)} %bitcast.24, bf16[8,128]{1,0:T(8,128)(2,1)S(1)} %bitcast.27, bf16[4,4096,128]{2,1,0:T(8,128)(2,1)S(1)} %bitcast.18), custom_call_target="tpu_custom_call" | custom-call | flops 67108864 | bytes 2097152 | tf_op jit(solution)/shard_map/resident/pallas_call | solution.py:292
  93.7 0.0 copy-start.5
  93.7 0.6 copy-done.5
  94.3 2.1 %resident.3.refs_1_ = f32[2,8,128]{2,1,0:T(8,128)S(1)} custom-call(s32[4]{0:T(128)S(1)} %bitcast.30, bf16[4,1024]{1,0:T(4,128)(2,1)S(1)} %bitcast.25, bf16[8,128]{1,0:T(8,128)(2,1)S(1)} %bitcast.28, bf16[4,4096,128]{2,1,0:T(8,128)(2,1)S(1)} %bitcast.19), custom_call_target="tpu_custom_call" | custom-call | flops 67108864 | bytes 2097152 | tf_op jit(solution)/shard_map/resident/pallas_call | solution.py:292
  96.4 0.0 copy-start.6
  96.4 0.6 copy-done.6
  97.0 0.0 all-to-all-done.3.got
  97.0 0.0 copy-start.11
  97.0 0.6 copy-done.11
  97.7 1.5 %merge.1 = bf16[4,1024]{1,0:T(4,128)(2,1)} custom-call(s32[4]{0:T(128)} %pad_add_fusion.meta, s32[2,8]{1,0:T(2,128)} %assign.7, f32[16,8,128]{2,1,0:T(8,128)} %copy-done.11, f32[2,8,128]{2,1,0:T(8,128)} %copy-done.5, f32[2,8,128]{2,1,0:T(8,128)} %copy-done.6), custom_call_target="tpu_custom_call" | custom-call | tf_op jit(solution)/shard_map/merge/pallas_call | solution.py:344
  (1 shorter events, 0.0 us)
Async XLA Ops:
  1.3 50.2 %collective-permute-start = (bf16[512,1024]{1,0:T(8,128)(2,1)S(1)}, bf16[512,1024]{1,0:T(8,128)(2,1)S(1)}, u32[]{:S(2)}, u32[]{:S(2)}) collective-permute-start(bf16[512,1024]{1,0:T(8,128)(2,1)S(1)} %dynamic-slice_bitcast_fusion), channel_id=1, source_target_pairs={{0,4},{1,5},{2,6},{3,7},{4,0},{5,1},{6,2},{7,3},{8,12},{9,13},{10,... | collective-permute-start | bytes 3145736 | tf_op jit(solution)/shard_map/ppermute | solution.py:250
  30.0 21.5 %copy-start.2 = (bf16[1,1024,1024]{2,1,0:T(8,128)(2,1)S(1)}, bf16[1,1024,1024]{2,1,0:T(8,128)(2,1)}, u32[]{:S(2)}) copy-start(bf16[1,1024,1024]{2,1,0:T(8,128)(2,1)} %param.7) | copy-start | bytes 6291460
  30.0 21.5 %copy-start.7 = (s32[4]{0:T(128)S(1)}, s32[4]{0:T(128)}, u32[]{:S(2)}) copy-start(s32[4]{0:T(128)} %pad_add_fusion.meta) | copy-start | bytes 52
  51.5 25.0 %copy-start = (bf16[8192,2,128]{2,1,0:T(2,128)(2,1)S(1)}, bf16[8192,2,128]{2,1,0:T(2,128)(2,1)}, u32[]{:S(2)}) copy-start(bf16[8192,2,128]{2,1,0:T(2,128)(2,1)} %param.8) | copy-start | bytes 12582916
  51.5 25.0 %copy-start.3 = (bf16[16,16,128]{2,1,0:T(8,128)(2,1)S(1)}, bf16[16,16,128]{2,1,0:T(8,128)(2,1)}, u32[]{:S(2)}) copy-start(bf16[16,16,128]{2,1,0:T(8,128)(2,1)} %all_to_all.20.got) | copy-start | bytes 196612
  51.5 25.0 %copy-start.9 = (s32[2,8]{1,0:T(2,128)S(1)}, s32[2,8]{1,0:T(2,128)}, u32[]{:S(2)}) copy-start(s32[2,8]{1,0:T(2,128)} %assign.7) | copy-start | bytes 196
  52.9 3.9 %collective-permute-start.1 = (f32[64,512]{1,0:T(8,128)S(1)}, f32[64,512]{1,0:T(8,128)S(1)}, u32[]{:S(2)}, u32[]{:S(2)}) collective-permute-start(f32[64,512]{1,0:T(8,128)S(1)} %score.1), channel_id=1, source_target_pairs={{0,1},{1,0},{2,3},{3,2},{4,5},{5,4},{6,7},{7,6},{8,9},{9,8},{10,11... | collective-permute-start | bytes 393224 | tf_op jit(solution)/shard_map/ppermute | solution.py:286
  56.9 5.4 %collective-permute-start.2 = (f32[64,512]{1,0:T(8,128)S(1)}, f32[64,512]{1,0:T(8,128)S(1)}, u32[]{:S(2)}, u32[]{:S(2)}) collective-permute-start(f32[64,512]{1,0:T(8,128)S(1)} %add.8.left), channel_id=1, source_target_pairs={{0,2},{1,3},{2,0},{3,1},{4,6},{5,7},{6,4},{7,5},{8,10},{9,11},{10,... | collective-permute-start | bytes 393224 | tf_op jit(solution)/shard_map/ppermute | solution.py:287
  76.5 12.8 %copy-start.4 = (bf16[1,4,1024]{2,1,0:T(4,128)(2,1)S(1)}, bf16[1,4,1024]{2,1,0:T(4,128)(2,1)}, u32[]{:S(2)}) copy-start(bf16[1,4,1024]{2,1,0:T(4,128)(2,1)} %param.10) | copy-start | bytes 24580
  76.5 12.8 %copy-start.8 = (bf16[1,4,2,128]{3,2,1,0:T(2,128)(2,1)S(1)}, bf16[1,4,2,128]{3,2,1,0:T(2,128)(2,1)}, u32[]{:S(2)}) copy-start(bf16[1,4,2,128]{3,2,1,0:T(2,128)(2,1)} %param.11) | copy-start | bytes 6148
  76.5 12.8 %copy-start.10 = (s32[1,4]{1,0:T(1,128)S(1)}, s32[1,4]{1,0:T(1,128)}, u32[]{:S(2)}) copy-start(s32[1,4]{1,0:T(1,128)} %param.12) | copy-start | bytes 52
  80.3 16.8 %all-to-all-start.3 = ((f32[16,8,128]{2,1,0:T(8,128)}), f32[16,8,128]{2,1,0:T(8,128)S(1)}, u32[]{:S(2)}, u32[]{:S(2)}) async-start(f32[16,8,128]{2,1,0:T(8,128)} %value.1), calls=%async_computation.3 | async-start | bytes 131072 | tf_op jit(solution)/shard_map/all_to_all | solution.py:342
  89.4 2.2 %copy-start.1 = (bf16[1,4,2048,2,128]{4,3,2,1,0:T(2,128)(2,1)S(1)}, bf16[1,4,2048,2,128]{4,3,2,1,0:T(2,128)(2,1)}, u32[]{:S(2)}) copy-start(bf16[1,4,2048,2,128]{4,3,2,1,0:T(2,128)(2,1)} %param.9) | copy-start | bytes 12582916
  93.7 0.6 copy-start.5
  96.4 0.6 copy-start.6
  97.0 0.6 copy-start.11

commit v2 on v1

v2 whole, which is shorter than its diff:
```python
import functools

import jax
import jax.numpy as jnp
from jax import lax
from jax.experimental import pallas as pl
from jax.experimental.pallas import tpu as pltpu
from jax.sharding import PartitionSpec as P

HD = 128
F32 = jnp.float32
BF16 = jnp.bfloat16
NEG = -1e30


def nt(a, b):
    return lax.dot_general(a, b, (((1,), (1,)), ((), ())), preferred_element_type=F32)


def nn(a, b):
    return jnp.dot(a, b, preferred_element_type=F32)


def split(x):
    hi = x.astype(BF16)
    lo = (x - hi.astype(F32)).astype(BF16)
    return hi, lo


def heads_of(row, groups):
    return jnp.concatenate([row[:, h * HD:(h + 1) * HD] for h in range(groups)], axis=0)


def spread(rows, cols, odd):
    r = lax.broadcasted_iota(jnp.int32, (rows, cols), 0)
    c = lax.broadcasted_iota(jnp.int32, (rows, cols), 1)
    return jnp.where(r == 2 * c + odd, 1.0, 0.0).astype(F32).astype(BF16)


def gather_t(rows, cols, odd):
    r = lax.broadcasted_iota(jnp.int32, (rows, cols), 0)
    c = lax.broadcasted_iota(jnp.int32, (rows, cols), 1)
    return jnp.where(c == 2 * r + odd, 1.0, 0.0).astype(F32).astype(BF16)


def own_of(packed):
    q = packed[0:8]
    k = packed[8:9]
    v = packed[9:10]
    return jnp.sum(q * k, axis=1, keepdims=True) * (HD ** -0.5), v


def send_kernel(assign, query, own, out, pick, mask):
    me, g = lax.axis_index("pool"), lax.axis_index("dp")
    rows = query.shape[0]
    n = assign.shape[1]
    q = query[...].astype(F32)
    kv = own[...].astype(F32)
    packed = []
    for j in range(rows):
        mine = heads_of(q[j:j + 1], q.shape[1] // HD)
        pad = jnp.zeros((16 - mine.shape[0] - 2, HD), F32)
        packed.append(jnp.concatenate([mine, kv[2 * j:2 * j + 2], pad], axis=0))
    for i in range(n):
        at = assign[1 - me, i] - g * rows
        value = packed[0]
        for j in range(1, rows):
            value = jnp.where(at == j, packed[j], value)
        value = value.astype(BF16)
        out[i] = value
        out[n + i] = value
    source = (1 - me) * n + assign[me, g] // rows
    slot = lax.broadcasted_iota(jnp.int32, pick.shape, 0)
    pick[...] = jnp.where(slot == source, 1.0, 0.0)
    slots = 2 * n
    slot = lax.broadcasted_iota(jnp.int32, mask.shape, 0)
    chosen = jnp.zeros(mask.shape, F32)
    for i in range(n):
        at = assign[1 - me, i] - g * rows
        target = jnp.where((at >= 0) & (at < rows), at * slots + (1 - me) * n + i, -1)
        chosen = jnp.where(slot == target, 1.0, chosen)
    mask[...] = chosen


def stage_kernel(odd, w, *refs):
    out = refs[-1]
    pick = gather_t(128, 256, odd)
    for b in range(out.shape[0] // 128):
        out[b * 128:(b + 1) * 128] = nn(pick, w[b * 256:(b + 1) * 256]).astype(BF16)


def fold_kernel(got, pick, w, out, mine):
    row = jnp.zeros(mine.shape, F32)
    for j in range(got.shape[0]):
        row = jnp.where(pick[j:j + 1] > 0.5, got[j].astype(F32), row)
    mine[...] = row
    d = out.shape[2]
    wide = nt(row[0:8].astype(BF16), w[...])
    for j in range(out.shape[0]):
        out[j] = wide[:, j * d:(j + 1) * d]


def score_kernel(qs, h, out):
    n, heads, d = qs.shape
    hi, lo = split(qs[...].reshape(n * heads, d))
    both = nt(jnp.concatenate([hi, lo], axis=0), h[...])
    out[...] = both[:n * heads] + both[n * heads:]


def mix_kernel(left, right, mine, h, first, second, values, out, scale_out, own_out, top_ref, total_ref):
    n, heads, d = out.shape
    t = lax.axis_index("tp")
    s = (left[...] + right[...]) * (HD ** -0.5)
    top = jnp.max(s, axis=1, keepdims=True)
    weights = jnp.exp(s - top)
    total = jnp.sum(weights, axis=1, keepdims=True)
    out[...] = nn(weights.astype(BF16), h[...]).reshape(n, heads, d)
    top_ref[...] = jnp.broadcast_to(top, top_ref.shape)
    total_ref[...] = jnp.broadcast_to(total, total_ref.shape)
    at = pl.ds(pl.multiple_of(t * heads, heads), heads)
    own_score, own_v = own_of(mine[...])
    here = top_ref[at, :]
    both = jnp.maximum(here, own_score)
    own_weight = jnp.exp(own_score - both)
    shrink = jnp.exp(here - both)
    whole = shrink * total_ref[at, :] + own_weight
    scale_out[...] = shrink / whole
    own_out[...] = own_weight.astype(BF16).astype(F32) * own_v / whole


def value_kernel(mixed, w, scale, own, out):
    n, heads, d = mixed.shape
    acc = jnp.zeros((2 * heads, HD), F32)
    for j in range(n):
        hi, lo = split(mixed[j])
        acc = acc + nn(jnp.concatenate([hi, lo], axis=0), w[d * j:d * (j + 1), :])
    done = (acc[:heads] + acc[heads:]) * scale[...] + own[...]
    for j in range(out.shape[0]):
        out[j] = done


def resident_kernel(first, lengths, query, own, kv, after, out):
    j = pl.program_id(0) + first
    live = lengths[j]
    rows = query.shape[0]
    wide = query[...].astype(F32)
    pairs = own[...].astype(F32)
    row = wide[0:1]
    ok = pairs[0:1]
    ov = pairs[1:2]
    for r in range(1, rows):
        row = jnp.where(j == r, wide[r:r + 1], row)
        ok = jnp.where(j == r, pairs[2 * r:2 * r + 1], ok)
        ov = jnp.where(j == r, pairs[2 * r + 1:2 * r + 2], ov)
    q = heads_of(row, query.shape[1] // HD)
    own_score = jnp.sum(q * ok, axis=1, keepdims=True) * (HD ** -0.5)
    s = nt(q.astype(BF16), kv[0]) * (HD ** -0.5)
    at = lax.broadcasted_iota(jnp.int32, s.shape, 1)
    valid = (at < 2 * live) & (at % 2 == 0)
    s = jnp.where(valid, s, NEG)
    top = jnp.maximum(jnp.max(s, axis=1, keepdims=True), own_score)
    weights = jnp.where(valid, jnp.exp(s - top), 0.0)
    own_weight = jnp.exp(own_score - top)
    total = jnp.sum(weights, axis=1, keepdims=True) + own_weight
    shifted = pltpu.roll(weights, 1, 1).astype(BF16)
    mixed = nn(shifted, kv[0]) + own_weight.astype(BF16).astype(F32) * ov
    out[0] = mixed / total


def merge_kernel(mask, got, *refs):
    out = refs[-1]
    n = got.shape[0]
    here = [part[k] for part in refs[:-1] for k in range(part.shape[0])]
    rows = []
    for j, value in enumerate(here):
        for i in range(n):
            value = jnp.where(mask[j * n + i:j * n + i + 1] > 0.5, got[i], value)
        rows.append(jnp.concatenate([value[h:h + 1] for h in range(value.shape[0])], axis=1))
    out[...] = jnp.concatenate(rows, axis=0).astype(BF16)


SMEM = pl.BlockSpec(memory_space=pltpu.SMEM)
VMEM = pl.BlockSpec(memory_space=pltpu.VMEM)
ANY = pl.BlockSpec(memory_space=pl.ANY)
MIB = 1024 * 1024


def shaped(shape, dtype):
    return jax.ShapeDtypeStruct(shape, dtype)


def call(kernel, limit, **kw):
    return pl.pallas_call(
        kernel, compiler_params=pltpu.CompilerParams(vmem_limit_bytes=limit * MIB), **kw
    )


def per_device(hidden, w_kv, cache, query, new_kv, lengths, assign):
    h = hidden[0]
    plen, dloc = h.shape
    rows, cap = cache.shape[1], cache.shape[2]
    heads = query.shape[2] // HD
    n_tp = lax.axis_size("tp")
    n_dp = lax.axis_size("dp")
    n_all = 2 * n_dp
    w = w_kv.reshape(w_kv.shape[0] * 2, HD)
    kv = cache.reshape(rows, cap * 2, HD)
    q_rows = query[0]
    own = new_kv[0].reshape(rows * 2, HD)

    sent, pick, mask = call(
        send_kernel,
        56,
        out_shape=[
            shaped((n_all, 16, HD), BF16),
            shaped((n_all, HD), F32),
            shaped((rows * n_all, HD), F32),
        ],
        in_specs=[SMEM, VMEM, VMEM],
        out_specs=[VMEM, VMEM, VMEM],
        name="send",
    )(assign, q_rows, own)
    def stage(odd, *after):
        return call(
            functools.partial(stage_kernel, odd),
            24,
            out_shape=shaped((w_kv.shape[0], HD), BF16),
            in_specs=[VMEM] + [ANY] * len(after),
            out_specs=VMEM,
            name="stage",
            cost_estimate=pl.CostEstimate(
                flops=4 * w.size * HD, bytes_accessed=3 * w.size, transcendentals=0
            ),
        )(w, *after)

    keys = stage(0)
    got = lax.all_to_all(sent, ("pool", "dp"), 0, 0, tiled=True)
    h, got = lax.optimization_barrier((h, got))

    folded, mine = call(
        fold_kernel,
        24,
        out_shape=[shaped((n_tp, heads, dloc), F32), shaped((16, HD), F32)],
        in_specs=[VMEM, VMEM, VMEM],
        out_specs=[VMEM, VMEM],
        name="fold",
    )(got, pick, keys)
    folded = lax.all_to_all(folded, "tp", 0, 0, tiled=True)

    score = call(
        score_kernel,
        24,
        out_shape=shaped((n_tp * heads, plen), F32),
        in_specs=[VMEM, VMEM],
        out_specs=VMEM,
        name="score",
    )(folded, h)

    def resident(first, after):
        return call(
            functools.partial(resident_kernel, first),
            24,
            grid=(2,),
            out_shape=shaped((2, heads, HD), F32),
            in_specs=[
                SMEM,
                VMEM,
                VMEM,
                pl.BlockSpec((1, cap * 2, HD), lambda i: (i + first, 0, 0)),
                ANY,
            ],
            out_specs=pl.BlockSpec((1, heads, HD), lambda i: (i, 0, 0)),
            name="resident",
            cost_estimate=pl.CostEstimate(
                flops=2 * 2 * 16 * cap * 2 * HD * 2, bytes_accessed=2 * cap * 2 * HD * 2, transcendentals=0
            ),
        )(lengths[0], q_rows, own, kv, after)

    def exchange(x, even, odd):
        pairs = []
        for g in range(n_dp):
            for t in range(n_tp):
                pairs.append((g * n_tp + t, g * n_tp + (even, odd)[g % 2](t)))
        return lax.ppermute(x, ("dp", "tp"), pairs)

    n_z = n_tp // 2

    def far(t):
        return (t + n_z) % n_tp

    def up(t):
        return t ^ 1

    def down(t):
        return t // n_z * n_z + n_z - 1 - t % n_z

    values = stage(1, score)
    first = resident(0, score)
    score = score + exchange(score, far, down)
    second = resident(2, score)
    score = score + exchange(score, up, far)
    twin = exchange(score, down, up)

    mixed, scale, own_part = call(
        mix_kernel,
        24,
        out_shape=[shaped((n_tp, heads, dloc), F32), shaped((heads, HD), F32), shaped((heads, HD), F32)],
        in_specs=[VMEM, VMEM, VMEM, VMEM, ANY, ANY, ANY],
        out_specs=[VMEM, VMEM, VMEM],
        scratch_shapes=[pltpu.VMEM((n_tp * heads, HD), F32), pltpu.VMEM((n_tp * heads, HD), F32)],
        name="mix",
    )(score, twin, mine, h, first, second, values)
    mixed = lax.all_to_all(mixed, "tp", 0, 0, tiled=True)

    done = call(
        value_kernel,
        24,
        out_shape=shaped((n_all, heads, HD), F32),
        in_specs=[VMEM, VMEM, VMEM, VMEM],
        out_specs=VMEM,
        name="value",
    )(mixed, values, scale, own_part)
    done = lax.all_to_all(done, ("pool", "dp"), 0, 0, tiled=True)

    merged = call(
        merge_kernel,
        24,
        out_shape=shaped((rows, heads * HD), BF16),
        in_specs=[VMEM, VMEM, VMEM, VMEM],
        out_specs=VMEM,
        name="merge",
    )(mask, done, first, second)
    return merged[None]


def solution(mesh):
    placed = (
        P("pool", "dp", "tp"),
        P(None, None, "tp"),
        P("pool", "dp", None, None, "tp"),
        P("pool", "dp", "tp"),
        P("pool", "dp", None, "tp"),
        P("pool", "dp"),
        P(),
    )
    return jax.shard_map(
        per_device, mesh=mesh, in_specs=placed, out_specs=P("pool", "dp", "tp"), check_vma=False
    )
```

time: 99.7 us -> 76.4 us (0.77)
  blocking collectives: 52.4 us -> 39.6 us
  Pallas kernels: 18.5 us -> 11.3 us
  waiting for transfers between devices: 7.56 us -> 14.3 us
  starting transfers between devices: 14.6 us -> 8.34 us
  local copies, waits for them, and re-layouts: 5.34 us -> 2.23 us
    all_to_all x1, blocking collectives: 22.9 us -> 12.5 us  [per_device(): done = lax.all_to_all(done, ('pool', 'dp'), 0, 0, tiled=True)]
    pallas_call x8 -> x10, Pallas kernels: 18.5 us -> 11.3 us  [the longest x2 4.3 us: resident(): call(functools.partial(resident_kernel, first), 24, grid=(2,), out_shape=...]
    ppermute x3, waiting for transfers between devices: 7.56 us -> 11.9 us  [exchange(): return lax.ppermute(x, ('dp', 'tp'), pairs)]
    ppermute x3, starting transfers between devices: 5.56 us -> 1.51 us  [exchange(): return lax.ppermute(x, ('dp', 'tp'), pairs)]
    all_to_all x1, waiting for transfers between devices: 0.01 us -> 2.39 us  [per_device(): got = lax.all_to_all(sent, ('pool', 'dp'), 0, 0, tiled=True)]
    all_to_all x1, starting transfers between devices: 9.06 us -> 6.83 us  [per_device(): got = lax.all_to_all(sent, ('pool', 'dp'), 0, 0, tiled=True)]
    unnamed x24 -> x18, local copies, waits for them, and re-layouts: 4.04 us -> 2.23 us
    all_to_all x1, blocking collectives: 16.3 us -> 14.9 us  [per_device(): folded = lax.all_to_all(folded, 'tp', 0, 0, tiled=True)]
  transfers between devices with their start and end apart: 4 -> 4, of which waited for: 2 -> 3; matrix products, arithmetic and copies ran while one was open for 1% -> 0% of each run, Pallas kernels for 10% -> 9%
where the time goes in v2:
time: 76.4 us; the launch traced here: 75.9 us
  blocking collectives  39.6 us (52%)
  waiting for transfers between devices  14.3 us (19%)
  Pallas kernels  11.3 us (15%)
  starting transfers between devices  8.34 us (11%)
  local copies, waits for them, and re-layouts  2.23 us (3%)
    all_to_all x1, blocking collectives, per_device(): folded = lax.all_to_all(folded, 'tp', 0, 0, tiled=True)  14.9 us
    all_to_all x1, blocking collectives, per_device(): done = lax.all_to_all(done, ('pool', 'dp'), 0, 0, tiled=True)  12.5 us
    all_to_all x1, blocking collectives, per_device(): mixed = lax.all_to_all(mixed, 'tp', 0, 0, tiled=True)  12.2 us
    ppermute x3, waiting for transfers between devices, exchange(): return lax.ppermute(x, ('dp', 'tp'), pairs)  11.9 us
    all_to_all x1, starting transfers between devices, per_device(): got = lax.all_to_all(sent, ('pool', 'dp'), 0, 0, tiled=True)  6.83 us
    pallas_call x2, Pallas kernels, resident(): call(functools.partial(resident_kernel, first), 24, grid=(2,), out_shape=...  4.3 us
    pallas_call x2, Pallas kernels, stage(): call(functools.partial(stage_kernel, odd), 24, out_shape=shaped((w_kv.sha...  2.48 us
    all_to_all x1, waiting for transfers between devices, per_device(): got = lax.all_to_all(sent, ('pool', 'dp'), 0, 0, tiled=True)  2.39 us
  transfers between devices with their start and end apart: 4, of which 3 were waited for; matrix products, arithmetic and copies ran while one was open for 0% of the time, Pallas kernels for 9%

profile of v2, /device:TPU:1, one launch (start us, length us, event | category | flops | bytes accessed | tf_op | source)
XLA Modules:
  0.0 75.9 jit_solution(14513285252680919357)
XLA Ops:
  0.0 1.4 %send.1 = (bf16[16,16,128]{2,1,0:T(8,128)(2,1)}, f32[16,128]{1,0:T(8,128)}, f32[64,128]{1,0:T(8,128)}) custom-call(s32[2,8]{1,0:T(2,128)} %assign.1, bf16[4,1024]{1,0:T(4,128)(2,1)} %bitcast.13, bf16[8,128]{1,0:T(8,128)(2,1)} %bitcast.16), custom_call_target="tpu_custom_call" | custom-call | tf_op jit(solution)/shard_map/send/pallas_call | solution.py:211
  1.4 6.8 %all-to-all-start = ((bf16[16,16,128]{2,1,0:T(8,128)(2,1)}), bf16[16,16,128]{2,1,0:T(8,128)(2,1)S(1)}, u32[]{:S(2)}, u32[]{:S(2)}) async-start(bf16[16,16,128]{2,1,0:T(8,128)(2,1)} %get-tuple-element.16), calls=%async_computation | async-start | bytes 131072 | tf_op jit(solution)/shard_map/all_to_all | solution.py:237
  8.2 0.0 copy-start
  8.2 2.2 %copy-done = bf16[8192,2,128]{2,1,0:T(2,128)(2,1)S(1)} copy-done((bf16[8192,2,128]{2,1,0:T(2,128)(2,1)S(1)}, bf16[8192,2,128]{2,1,0:T(2,128)(2,1)}, u32[]{:S(2)}) %copy-start) | copy-done | bytes 4194328
  10.4 0.0 copy-start.7
  10.4 1.2 %stage.2.w = bf16[8192,128]{1,0:T(8,128)(2,1)S(1)} custom-call(bf16[16384,128]{1,0:T(8,128)(2,1)S(1)} %bitcast.7), custom_call_target="tpu_custom_call" | custom-call | flops 1073741824 | bytes 6291456 | tf_op jit(solution)/shard_map/stage/pallas_call | solution.py:224
  11.7 2.4 %all-to-all-done.got = bf16[16,16,128]{2,1,0:T(8,128)(2,1)S(1)} async-done(((bf16[16,16,128]{2,1,0:T(8,128)(2,1)}), bf16[16,16,128]{2,1,0:T(8,128)(2,1)S(1)}, u32[]{:S(2)}, u32[]{:S(2)}) %all-to-all-start) | async-done | bytes 65568 | tf_op jit(solution)/shard_map/all_to_all | solution.py:237
  14.1 0.0 copy-start.3
  14.1 0.0 copy-done.7
  14.1 0.6 fold.1
  14.7 0.0 copy-start.4
  14.7 14.9 %all_to_all.20.qs = f32[8,8,1024]{2,1,0:T(8,128)S(1)} all-to-all(f32[8,8,1024]{2,1,0:T(8,128)S(1)} %get-tuple-element.19), channel_id=1, replica_groups=mesh['pool'=2,'dp'=8,'tp'=8] {'tp'}, dimensions={0} | all-to-all | bytes 524288 | tf_op jit(solution)/shard_map/all_to_all | solution.py:248
  29.6 0.0 copy-done.3
  29.6 0.0 copy-start.2
  29.6 0.0 copy-start.6
  29.6 0.0 copy-start.8
  29.6 0.8 %score.1.after.refs_0_ = f32[64,1024]{1,0:T(8,128)S(1)} custom-call(f32[8,8,1024]{2,1,0:T(8,128)S(1)} %all_to_all.20.qs, bf16[1024,1024]{1,0:T(8,128)(2,1)S(1)} %bitcast.11), custom_call_target="tpu_custom_call" | custom-call | tf_op jit(solution)/shard_map/score/pallas_call | solution.py:250
  30.4 1.0 %collective-permute-start = (f32[64,1024]{1,0:T(8,128)S(1)}, f32[64,1024]{1,0:T(8,128)S(1)}, u32[]{:S(2)}, u32[]{:S(2)}) collective-permute-start(f32[64,1024]{1,0:T(8,128)S(1)} %score.1.after.refs_0_), channel_id=1, source_target_pairs={{0,4},{1,5},{2,6},{3,7},{4,0},{5,1},{6,2},{7,3},{8,11},{9,10},{10,... | collective-permute-start | bytes 786440 | tf_op jit(solution)/shard_map/ppermute | solution.py:284
  31.4 5.5 %collective-permute-done = f32[64,1024]{1,0:T(8,128)S(1)} collective-permute-done((f32[64,1024]{1,0:T(8,128)S(1)}, f32[64,1024]{1,0:T(8,128)S(1)}, u32[]{:S(2)}, u32[]{:S(2)}) %collective-permute-start) | collective-permute-done | bytes 262176 | tf_op jit(solution)/shard_map/ppermute | solution.py:284
  37.0 0.5 collective-permute-start.1
  37.4 6.4 %collective-permute-done.1 = f32[64,1024]{1,0:T(8,128)S(1)} collective-permute-done((f32[64,1024]{1,0:T(8,128)S(1)}, f32[64,1024]{1,0:T(8,128)S(1)}, u32[]{:S(2)}, u32[]{:S(2)}) %collective-permute-start.1) | collective-permute-done | bytes 262176 | tf_op jit(solution)/shard_map/ppermute | solution.py:284
  43.8 0.1 collective-permute-start.2
  43.9 0.0 copy-done.4
  43.9 0.0 copy-done.2
  43.9 0.0 copy-done.6
  43.9 0.0 copy-done.8
  44.0 0.0 copy-start.1
  44.0 2.1 %resident.2.first.refs_0_ = f32[2,8,128]{2,1,0:T(8,128)S(1)} custom-call(s32[4]{0:T(128)S(1)} %bitcast.19, bf16[4,1024]{1,0:T(4,128)(2,1)S(1)} %bitcast.14, bf16[8,128]{1,0:T(8,128)(2,1)S(1)} %bitcast.17, bf16[4,4096,128]{2,1,0:T(8,128)(2,1)S(1)} %bitcast.9, f32[64,1024]{1,0:T(8,128)S(1)} %score.1.after.refs_0_), custom_call_target="tpu_custom_call" | custom-call | flops 67108864 | bytes 2097152 | tf_op jit(solution)/shard_map/resident/pallas_call | solution.py:260
  46.1 0.0 copy-done.1
  46.2 1.2 %stage.3.values.w = bf16[8192,128]{1,0:T(8,128)(2,1)S(1)} custom-call(bf16[16384,128]{1,0:T(8,128)(2,1)S(1)} %bitcast.8, f32[64,1024]{1,0:T(8,128)S(1)} %score.1.after.refs_0_), custom_call_target="tpu_custom_call" | custom-call | flops 1073741824 | bytes 6291456 | tf_op jit(solution)/shard_map/stage/pallas_call | solution.py:224
  47.4 2.2 %resident.3.second.refs_1_ = f32[2,8,128]{2,1,0:T(8,128)S(1)} custom-call(s32[4]{0:T(128)S(1)} %bitcast.20, bf16[4,1024]{1,0:T(4,128)(2,1)S(1)} %bitcast.15, bf16[8,128]{1,0:T(8,128)(2,1)S(1)} %bitcast.18, bf16[4,4096,128]{2,1,0:T(8,128)(2,1)S(1)} %bitcast.10, f32[64,1024]{1,0:T(8,128)S(1)} %add.6.after), custom_call_target="tpu_custom_call" | custom-call | flops 67108864 | bytes 2097152 | tf_op jit(solution)/shard_map/resident/pallas_call | solution.py:260
  49.6 0.0 collective-permute-done.2.right
  49.6 0.6 mix.1
  50.1 0.0 copy-start.5
  50.1 12.2 %all_to_all.21.mixed = f32[8,8,1024]{2,1,0:T(8,128)S(1)} all-to-all(f32[8,8,1024]{2,1,0:T(8,128)S(1)} %get-tuple-element.22), channel_id=1, replica_groups=mesh['pool'=2,'dp'=8,'tp'=8] {'tp'}, dimensions={0} | all-to-all | bytes 524288 | tf_op jit(solution)/shard_map/all_to_all | solution.py:313
  62.3 0.4 value.1
  62.7 12.5 %all_to_all.22.got = f32[16,8,128]{2,1,0:T(8,128)S(1)} all-to-all(f32[16,8,128]{2,1,0:T(8,128)S(1)} %value.1), channel_id=1, replica_groups=mesh['pool'=2,'dp'=8,'tp'=8] {'pool','dp'}, dimensions={0} | all-to-all | bytes 131072 | tf_op jit(solution)/shard_map/all_to_all | solution.py:323
  75.3 0.0 copy-done.5
  75.3 0.7 merge.1
  (2 shorter events, 0.1 us)
Async XLA Ops:
  1.4 12.7 %all-to-all-start = ((bf16[16,16,128]{2,1,0:T(8,128)(2,1)}), bf16[16,16,128]{2,1,0:T(8,128)(2,1)S(1)}, u32[]{:S(2)}, u32[]{:S(2)}) async-start(bf16[16,16,128]{2,1,0:T(8,128)(2,1)} %get-tuple-element.16), calls=%async_computation | async-start | bytes 131072 | tf_op jit(solution)/shard_map/all_to_all | solution.py:237
  8.2 2.2 %copy-start = (bf16[8192,2,128]{2,1,0:T(2,128)(2,1)S(1)}, bf16[8192,2,128]{2,1,0:T(2,128)(2,1)}, u32[]{:S(2)}) copy-start(bf16[8192,2,128]{2,1,0:T(2,128)(2,1)} %param.8) | copy-start | bytes 12582916
  10.4 3.6 %copy-start.7 = (f32[16,128]{1,0:T(8,128)S(1)}, f32[16,128]{1,0:T(8,128)}, u32[]{:S(2)}) copy-start(f32[16,128]{1,0:T(8,128)} %get-tuple-element.18.pick) | copy-start | bytes 24580
  14.1 15.5 %copy-start.3 = (bf16[1,1024,1024]{2,1,0:T(8,128)(2,1)S(1)}, bf16[1,1024,1024]{2,1,0:T(8,128)(2,1)}, u32[]{:S(2)}) copy-start(bf16[1,1024,1024]{2,1,0:T(8,128)(2,1)} %param.7) | copy-start | bytes 6291460
  14.7 29.2 %copy-start.4 = (bf16[1,4,1024]{2,1,0:T(4,128)(2,1)S(1)}, bf16[1,4,1024]{2,1,0:T(4,128)(2,1)}, u32[]{:S(2)}) copy-start(bf16[1,4,1024]{2,1,0:T(4,128)(2,1)} %param.10) | copy-start | bytes 24580
  29.6 14.3 %copy-start.2 = (bf16[1,4,2048,2,128]{4,3,2,1,0:T(2,128)(2,1)S(1)}, bf16[1,4,2048,2,128]{4,3,2,1,0:T(2,128)(2,1)}, u32[]{:S(2)}) copy-start(bf16[1,4,2048,2,128]{4,3,2,1,0:T(2,128)(2,1)} %param.9) | copy-start | bytes 12582916
  29.6 14.3 %copy-start.6 = (bf16[1,4,2,128]{3,2,1,0:T(2,128)(2,1)S(1)}, bf16[1,4,2,128]{3,2,1,0:T(2,128)(2,1)}, u32[]{:S(2)}) copy-start(bf16[1,4,2,128]{3,2,1,0:T(2,128)(2,1)} %param.11) | copy-start | bytes 6148
  29.6 14.3 %copy-start.8 = (s32[1,4]{1,0:T(1,128)S(1)}, s32[1,4]{1,0:T(1,128)}, u32[]{:S(2)}) copy-start(s32[1,4]{1,0:T(1,128)} %param.12) | copy-start | bytes 52
  30.4 6.5 %collective-permute-start = (f32[64,1024]{1,0:T(8,128)S(1)}, f32[64,1024]{1,0:T(8,128)S(1)}, u32[]{:S(2)}, u32[]{:S(2)}) collective-permute-start(f32[64,1024]{1,0:T(8,128)S(1)} %score.1.after.refs_0_), channel_id=1, source_target_pairs={{0,4},{1,5},{2,6},{3,7},{4,0},{5,1},{6,2},{7,3},{8,11},{9,10},{10,... | collective-permute-start | bytes 786440 | tf_op jit(solution)/shard_map/ppermute | solution.py:284
  37.0 6.8 %collective-permute-start.1 = (f32[64,1024]{1,0:T(8,128)S(1)}, f32[64,1024]{1,0:T(8,128)S(1)}, u32[]{:S(2)}, u32[]{:S(2)}) collective-permute-start(f32[64,1024]{1,0:T(8,128)S(1)} %add.6.after), channel_id=1, source_target_pairs={{0,1},{1,0},{2,3},{3,2},{4,5},{5,4},{6,7},{7,6},{8,12},{9,13},{10,... | collective-permute-start | bytes 786440 | tf_op jit(solution)/shard_map/ppermute | solution.py:284
  43.8 5.7 %collective-permute-start.2 = (f32[64,1024]{1,0:T(8,128)S(1)}, f32[64,1024]{1,0:T(8,128)S(1)}, u32[]{:S(2)}, u32[]{:S(2)}) collective-permute-start(f32[64,1024]{1,0:T(8,128)S(1)} %add.7.left), channel_id=1, source_target_pairs={{0,3},{1,2},{2,1},{3,0},{4,7},{5,6},{6,5},{7,4},{8,9},{9,8},{10,11... | collective-permute-start | bytes 786440 | tf_op jit(solution)/shard_map/ppermute | solution.py:284
  44.0 2.2 %copy-start.1 = (bf16[8192,2,128]{2,1,0:T(2,128)(2,1)S(1)}, bf16[8192,2,128]{2,1,0:T(2,128)(2,1)}, u32[]{:S(2)}) copy-start(bf16[8192,2,128]{2,1,0:T(2,128)(2,1)} %param.8) | copy-start | bytes 12582916
  50.1 25.1 %copy-start.5 = (f32[64,128]{1,0:T(8,128)S(1)}, f32[64,128]{1,0:T(8,128)}, u32[]{:S(2)}) copy-start(f32[64,128]{1,0:T(8,128)} %get-tuple-element.15.mask) | copy-start | bytes 98308
